TPU v7x, 256 devices: a whole 4x4x8 slice. The times are simulated.
256 devices in a mesh: seq: 16 (over x_lo, z), cfg: 16 (over y, x_hi, core).
Axes of the slice: x: 4 (x_hi: 2, x_lo: 2; x = x_hi * 2 + x_lo), y: 4, z: 8, core: 2. Of those that a mesh axis runs over, the one named last changes fastest.
Arguments:
- query_states: bfloat16 [16, 1536, 4096], P('cfg', 'seq'), may hold values from -8 to 8
- key_states: bfloat16 [16, 9216, 4096], P('cfg', 'seq'), may hold values from -8 to 8
- value_states: bfloat16 [16, 9216, 4096], P('cfg', 'seq'), may hold values from -6 to 6
- tile_pattern: int32 [8, 28], replicated, may hold values from -1 to 47, as said below
- strength: float32 [16], replicated, may hold values from 1 to 8
- partner: int32 [16], replicated, may hold values from 0 to 15, as said below
Outputs:
- guided: bfloat16 [16, 1536, 4096], P('cfg', 'seq')
Inputs may be any that keep to these rules, and one draw needn't show every extreme that they name: `tile_pattern`: each row holds 27 distinct tile numbers, those of a block of 3 x 3 x 3 neighbouring tiles that contains the row's own tile, and one entry -1 at some position. partner[partner[m]] = m and partner[m] != m.
All inputs are finite; a program needn't handle non-finite values.
Results may differ from a plain program's by a relative error of at most 0.0057.
Values may be sent and summed in bfloat16 or wider, within the bound.
A program may use at most 128 MiB of HBM per device.

v0:
```python
import math

import jax
import jax.numpy as jnp
from jax import lax
from jax.sharding import PartitionSpec as P

HEAD_DIM = 128
TILE_T = 6
TILE_H = 8
TILE_W = 4


def head_attention(query_head, key_head, value_head, tile_index, is_valid):
    query_tile_count = tile_index.shape[0]
    tile_size = TILE_T * TILE_H * TILE_W
    head_size = query_head.shape[1]
    slot_count = tile_index.shape[1]
    tile_count = key_head.shape[0] // tile_size
    group_count = query_tile_count // 4
    score_scale = 1.0 / math.sqrt(head_size)
    query_tiles = query_head.reshape(group_count, 4, tile_size, head_size)
    key_tiles = key_head.reshape(tile_count, tile_size, head_size)
    value_tiles = value_head.reshape(tile_count, tile_size, head_size)
    index_groups = tile_index.reshape(group_count, 4, slot_count)
    valid_groups = is_valid.reshape(group_count, 4, slot_count)

    def tile_block(inputs):
        query_block, index_block, valid_block = inputs
        key_block = jnp.take(key_tiles, index_block, axis=0)
        value_block = jnp.take(value_tiles, index_block, axis=0)
        scores = (
            jnp.einsum("iqd,iskd->iqsk", query_block, key_block, preferred_element_type=jnp.float32)
            * score_scale
        )
        scores = jnp.where(valid_block[:, None, :, None], scores, -1e30)
        maximum = jnp.max(scores, axis=(2, 3), keepdims=True)
        exponent = jnp.exp(scores - maximum)
        totals = jnp.sum(exponent, axis=(2, 3))
        weights = exponent.astype(jnp.bfloat16)
        attended = (
            jnp.einsum("iqsk,iskd->iqd", weights, value_block, preferred_element_type=jnp.float32)
            / totals[:, :, None]
        )
        return attended.astype(jnp.bfloat16)

    outputs = lax.map(tile_block, (query_tiles, index_groups, valid_groups))
    return outputs.reshape(query_tile_count * tile_size, head_size)


def combine(grouped, strength, partner):
    members = grouped.shape[0]
    onehot = (partner[:, None] == jnp.arange(members, dtype=jnp.int32)[None, :]).astype(
        jnp.bfloat16
    )
    partner_rows = jnp.einsum("mn,n...->m...", onehot, grouped, preferred_element_type=jnp.float32)
    strength_col = strength.reshape((members,) + (1,) * (grouped.ndim - 1))
    return (partner_rows + strength_col * (grouped.astype(jnp.float32) - partner_rows)).astype(
        jnp.bfloat16
    )


def body(query_states, key_states, value_states, tile_pattern, strength, partner):
    seq_count = lax.axis_size("seq")
    own_rows = query_states.shape[1]
    feature_width = query_states.shape[2]
    head_size = HEAD_DIM
    heads_here = feature_width // (seq_count * head_size)
    is_valid = tile_pattern >= 0
    tile_index = jnp.maximum(tile_pattern, 0)

    def split_heads(states):
        return states.reshape(1, states.shape[1], seq_count, heads_here, head_size)

    def flatten_heads(states):
        return jnp.moveaxis(states[0, :, 0], 1, 0)

    def one_head(triple_head):
        return head_attention(triple_head[0], triple_head[1], triple_head[2], tile_index, is_valid)

    outputs = lax.map(
        one_head,
        (
            flatten_heads(
                lax.all_to_all(
                    split_heads(query_states), "seq", split_axis=2, concat_axis=1, tiled=True
                )
            ),
            flatten_heads(
                lax.all_to_all(
                    split_heads(key_states), "seq", split_axis=2, concat_axis=1, tiled=True
                )
            ),
            flatten_heads(
                lax.all_to_all(
                    split_heads(value_states), "seq", split_axis=2, concat_axis=1, tiled=True
                )
            ),
        ),
    )
    attended = jnp.moveaxis(outputs, 0, 1)[None, :, None]
    token_major = lax.all_to_all(attended, "seq", split_axis=1, concat_axis=2, tiled=True)
    flattened = token_major.reshape(1, own_rows, feature_width)
    grouped = lax.all_to_all(flattened, "cfg", split_axis=1, concat_axis=0, tiled=True)
    combined = combine(grouped, strength, partner)
    guided = lax.all_to_all(combined, "cfg", split_axis=0, concat_axis=1, tiled=True)
    return guided


def solution(mesh):
    return jax.shard_map(
        body,
        mesh=mesh,
        in_specs=(
            P("cfg", "seq", None),
            P("cfg", "seq", None),
            P("cfg", "seq", None),
            P(),
            P(),
            P(),
        ),
        out_specs=P("cfg", "seq", None),
        check_vma=False,
    )
```

profile of v0, /device:TPU:1, one launch (start us, length us, event | category | flops | bytes accessed | tf_op | source)
XLA Modules:
  0.0 518.7 jit_solution(6460993871026822015)
XLA Ops:
  3.7 10.0 %all-to-all-start = ((bf16[1,96,16,2,128]{4,1,3,0,2:T(8,128)(2,1)}), bf16[1,96,16,2,128]{4,1,3,0,2:T(8,128)(2,1)S(1)}, u32[]{:S(2)}, u32[]{:S(2)}) async-start(bf16[1,96,16,2,128]{4,1,3,0,2:T(8,128)(2,1)} %copy.27), calls=%async_computation | async-start | bytes 1572864 | tf_op jit(solution)/shard_map/all_to_all | solution.py:85
  13.8 8.7 %reshape.55 = bf16[1,576,16,2,128]{4,3,2,1,0:T(2,128)(2,1)} reshape(bf16[1,576,4096]{2,1,0:T(8,128)(2,1)} %param.13) | data formatting | bytes 9437184 | tf_op jit(solution)/shard_map/reshape | solution.py:73
  22.5 6.4 %copy.29 = bf16[1,576,16,2,128]{4,1,3,0,2:T(8,128)(2,1)} copy(bf16[1,576,16,2,128]{4,3,2,1,0:T(2,128)(2,1)} %reshape.55) | data formatting | bytes 9437184 | tf_op jit(solution)/shard_map/reshape | solution.py:73
  33.6 6.3 %all-to-all-start.1 = ((bf16[1,576,16,2,128]{4,1,3,0,2:T(8,128)(2,1)}), bf16[1,576,16,2,128]{4,1,3,0,2:T(8,128)(2,1)}, u32[]{:S(2)}, u32[]{:S(2)}) async-start(bf16[1,576,16,2,128]{4,1,3,0,2:T(8,128)(2,1)} %copy.29), calls=%async_computation.1 | async-start | bytes 9437184 | tf_op jit(solution)/shard_map/all_to_all | solution.py:90
  39.9 8.7 %reshape.56 = bf16[1,576,16,2,128]{4,3,2,1,0:T(2,128)(2,1)} reshape(bf16[1,576,4096]{2,1,0:T(8,128)(2,1)} %param.14) | data formatting | bytes 9437184 | tf_op jit(solution)/shard_map/reshape | solution.py:73
  48.6 6.3 %copy.31 = bf16[1,576,16,2,128]{4,1,3,0,2:T(8,128)(2,1)} copy(bf16[1,576,16,2,128]{4,3,2,1,0:T(2,128)(2,1)} %reshape.56) | data formatting | bytes 9437184 | tf_op jit(solution)/shard_map/reshape | solution.py:73
  54.9 90.9 %all-to-all-done.1 = bf16[1,576,16,2,128]{4,1,3,0,2:T(8,128)(2,1)} async-done(((bf16[1,576,16,2,128]{4,1,3,0,2:T(8,128)(2,1)}), bf16[1,576,16,2,128]{4,1,3,0,2:T(8,128)(2,1)}, u32[]{:S(2)}, u32[]{:S(2)}) %all-to-all-start.1) | async-done | bytes 4718624 | tf_op jit(solution)/shard_map/all_to_all | solution.py:90
  145.9 9.0 %all-to-all-start.2 = ((bf16[1,576,16,2,128]{4,1,3,0,2:T(8,128)(2,1)}), bf16[1,576,16,2,128]{4,1,3,0,2:T(8,128)(2,1)}, u32[]{:S(2)}, u32[]{:S(2)}) async-start(bf16[1,576,16,2,128]{4,1,3,0,2:T(8,128)(2,1)} %copy.31), calls=%async_computation.2 | async-start | bytes 9437184 | tf_op jit(solution)/shard_map/all_to_all | solution.py:95
  160.7 100.0 %all-to-all-done.2 = bf16[1,576,16,2,128]{4,1,3,0,2:T(8,128)(2,1)} async-done(((bf16[1,576,16,2,128]{4,1,3,0,2:T(8,128)(2,1)}), bf16[1,576,16,2,128]{4,1,3,0,2:T(8,128)(2,1)}, u32[]{:S(2)}, u32[]{:S(2)}) %all-to-all-start.2) | async-done | bytes 4718624 | tf_op jit(solution)/shard_map/all_to_all | solution.py:95
  265.6 157.8 %while.21 = (s32[]{:T(128)}, bf16[2,1536,128]{2,1,0:T(8,128)(2,1)}, bf16[2,1536,128]{2,1,0:T(8,128)(2,1)}, s32[8,28]{1,0:T(8,128)S(1)}, pred[8,28]{1,0:T(8,128)(...) while((s32[]{:T(128)}, bf16[2,1536,128]{2,1,0:T(8,128)(2,1)}, ...), condition=%wide.region_5.7_spmd, body=%wide.region_0.6_spmd.sunk | while | flops 2165047552 | bytes 185232832 | solution.py:81
  269.2 73.5 %while.22 = (s32[]{:T(128)}, bf16[2,4,192,128]{3,2,1,0:T(8,128)(2,1)}, pred[2,4,28]{2,1,0:T(4,128)(4,1)S(1)}, bf16[2,4,192,128]{3,2,1,0:T(8,128)(2,1)S(1)}, s32[...) while((s32[]{:T(128)}, ...), condition=%wide.region_4.5_spmd, body=%wide.region_1.4_spmd.sunk | while | flops 2165047552 | bytes 171076336 | solution.py:47
  273.1 7.2 %fusion.56 = (f32[4,192]{1,0:T(4,128)S(1)}, f32[4,192,28,192]{1,3,2,0:T(8,128)S(1)}) fusion(pred[4,28]{1,0:T(4,128)(4,1)S(1)} %dynamic-slice_bitcast_fusion.2, bf16[4,28,192,128]{3,2,1,0:T(8,128)(2,1)} %bitcast.101, pred[4,28]{1,0:T(4,128)(4,1)S(1)} %get-tuple-element.227, bf16[2,4,192,128]{3,2,1,0:T(8,128)(2,1)S(1)} %get-tuple-element.249, ...), kind=kOutput, calls=%fused_computation.4.clone.1 | convolution fusion | flops 1072102656 | bytes 22220804 | tf_op jit(solution)/shard_map/while/body/eval_jaxpr/while/body/eval_jaxpr/iqd,iskd->iqsk/dot_general | solution.py:33
  280.4 5.7 %fusion.57 = f32[4,192]{1,0:T(4,128)S(1)} fusion(f32[4,192,28,192]{1,3,2,0:T(8,128)S(1)} %get-tuple-element.228, f32[4,192]{1,0:T(4,128)S(1)} %get-tuple-element.229, pred[4,28]{1,0:T(4,128)(4,1)S(1)} %dynamic-slice_bitcast_fusion.2), kind=kLoop, calls=%fused_computation.5.clone.1 | loop fusion | flops 16514304 | bytes 16521328 | tf_op jit(solution)/shard_map/while/body/eval_jaxpr/while/body/eval_jaxpr/reduce_sum | solution.py:39
  287.7 5.5 %gather_fusion = bf16[112,192,128]{2,1,0:T(8,128)(2,1)} fusion(bf16[48,192,128]{2,1,0:T(8,128)(2,1)} %get-tuple-element.252, s32[1024]{0:T(1024)S(1)} %pad_clamp_fusion.2), kind=kCustom, calls=%fused_computation.1.clone.clone.1 | custom fusion | bytes 11010496 | tf_op jit(solution)/shard_map/while/body/eval_jaxpr/while/body/eval_jaxpr/jit(_take)/gather | solution.py:31
  293.2 12.0 %fusion.58 = bf16[2,4,192,128]{3,2,1,0:T(8,128)(2,1)S(1)} fusion(bf16[2,4,192,128]{3,2,1,0:T(8,128)(2,1)S(1)} %copy-done.3, s32[]{:T(128)} %get-tuple-element.238, bf16[4,28,192,128]{3,2,1,0:T(8,128)(2,1)} %bitcast.100, pred[4,28]{1,0:T(4,128)(4,1)S(1)} %get-tuple-element.227, f32[4,192,28,192]{1,3,2,0:T(8,128)} %copy-done, ...), kind=kOutput, calls=%fused_computation.20.clone.1 | convolution fusion | flops 1076428800 | bytes 22225924 | tf_op jit(solution)/shard_map/while/body/eval_jaxpr/while/body/eval_jaxpr/iqsk,iskd->iqd/dot_general | solution.py:42
  309.9 7.2 %fusion.56 = (f32[4,192]{1,0:T(4,128)S(1)}, f32[4,192,28,192]{1,3,2,0:T(8,128)S(1)}) fusion(pred[4,28]{1,0:T(4,128)(4,1)S(1)} %dynamic-slice_bitcast_fusion.2, bf16[4,28,192,128]{3,2,1,0:T(8,128)(2,1)} %bitcast.101, pred[4,28]{1,0:T(4,128)(4,1)S(1)} %get-tuple-element.227, bf16[2,4,192,128]{3,2,1,0:T(8,128)(2,1)S(1)} %get-tuple-element.249, ...), kind=kOutput, calls=%fused_computation.4.clone.1 | convolution fusion | flops 1072102656 | bytes 22220804 | tf_op jit(solution)/shard_map/while/body/eval_jaxpr/while/body/eval_jaxpr/iqd,iskd->iqsk/dot_general | solution.py:33
  317.1 5.7 %fusion.57 = f32[4,192]{1,0:T(4,128)S(1)} fusion(f32[4,192,28,192]{1,3,2,0:T(8,128)S(1)} %get-tuple-element.228, f32[4,192]{1,0:T(4,128)S(1)} %get-tuple-element.229, pred[4,28]{1,0:T(4,128)(4,1)S(1)} %dynamic-slice_bitcast_fusion.2), kind=kLoop, calls=%fused_computation.5.clone.1 | loop fusion | flops 16514304 | bytes 16521328 | tf_op jit(solution)/shard_map/while/body/eval_jaxpr/while/body/eval_jaxpr/reduce_sum | solution.py:39
  324.4 5.5 %gather_fusion = bf16[112,192,128]{2,1,0:T(8,128)(2,1)} fusion(bf16[48,192,128]{2,1,0:T(8,128)(2,1)} %get-tuple-element.252, s32[1024]{0:T(1024)S(1)} %pad_clamp_fusion.2), kind=kCustom, calls=%fused_computation.1.clone.clone.1 | custom fusion | bytes 11010496 | tf_op jit(solution)/shard_map/while/body/eval_jaxpr/while/body/eval_jaxpr/jit(_take)/gather | solution.py:31
  329.9 12.0 %fusion.58 = bf16[2,4,192,128]{3,2,1,0:T(8,128)(2,1)S(1)} fusion(bf16[2,4,192,128]{3,2,1,0:T(8,128)(2,1)S(1)} %copy-done.3, s32[]{:T(128)} %get-tuple-element.238, bf16[4,28,192,128]{3,2,1,0:T(8,128)(2,1)} %bitcast.100, pred[4,28]{1,0:T(4,128)(4,1)S(1)} %get-tuple-element.227, f32[4,192,28,192]{1,3,2,0:T(8,128)} %copy-done, ...), kind=kOutput, calls=%fused_computation.20.clone.1 | convolution fusion | flops 1076428800 | bytes 22225924 | tf_op jit(solution)/shard_map/while/body/eval_jaxpr/while/body/eval_jaxpr/iqsk,iskd->iqd/dot_general | solution.py:42
  348.1 73.5 %while.22 = (s32[]{:T(128)}, bf16[2,4,192,128]{3,2,1,0:T(8,128)(2,1)}, pred[2,4,28]{2,1,0:T(4,128)(4,1)S(1)}, bf16[2,4,192,128]{3,2,1,0:T(8,128)(2,1)S(1)}, s32[...) while((s32[]{:T(128)}, ...), condition=%wide.region_4.5_spmd, body=%wide.region_1.4_spmd.sunk | while | flops 2165047552 | bytes 171076336 | solution.py:47
  352.0 7.2 %fusion.56 = (f32[4,192]{1,0:T(4,128)S(1)}, f32[4,192,28,192]{1,3,2,0:T(8,128)S(1)}) fusion(pred[4,28]{1,0:T(4,128)(4,1)S(1)} %dynamic-slice_bitcast_fusion.2, bf16[4,28,192,128]{3,2,1,0:T(8,128)(2,1)} %bitcast.101, pred[4,28]{1,0:T(4,128)(4,1)S(1)} %get-tuple-element.227, bf16[2,4,192,128]{3,2,1,0:T(8,128)(2,1)S(1)} %get-tuple-element.249, ...), kind=kOutput, calls=%fused_computation.4.clone.1 | convolution fusion | flops 1072102656 | bytes 22220804 | tf_op jit(solution)/shard_map/while/body/eval_jaxpr/while/body/eval_jaxpr/iqd,iskd->iqsk/dot_general | solution.py:33
  359.3 5.7 %fusion.57 = f32[4,192]{1,0:T(4,128)S(1)} fusion(f32[4,192,28,192]{1,3,2,0:T(8,128)S(1)} %get-tuple-element.228, f32[4,192]{1,0:T(4,128)S(1)} %get-tuple-element.229, pred[4,28]{1,0:T(4,128)(4,1)S(1)} %dynamic-slice_bitcast_fusion.2), kind=kLoop, calls=%fused_computation.5.clone.1 | loop fusion | flops 16514304 | bytes 16521328 | tf_op jit(solution)/shard_map/while/body/eval_jaxpr/while/body/eval_jaxpr/reduce_sum | solution.py:39
  366.6 5.5 %gather_fusion = bf16[112,192,128]{2,1,0:T(8,128)(2,1)} fusion(bf16[48,192,128]{2,1,0:T(8,128)(2,1)} %get-tuple-element.252, s32[1024]{0:T(1024)S(1)} %pad_clamp_fusion.2), kind=kCustom, calls=%fused_computation.1.clone.clone.1 | custom fusion | bytes 11010496 | tf_op jit(solution)/shard_map/while/body/eval_jaxpr/while/body/eval_jaxpr/jit(_take)/gather | solution.py:31
  372.1 12.0 %fusion.58 = bf16[2,4,192,128]{3,2,1,0:T(8,128)(2,1)S(1)} fusion(bf16[2,4,192,128]{3,2,1,0:T(8,128)(2,1)S(1)} %copy-done.3, s32[]{:T(128)} %get-tuple-element.238, bf16[4,28,192,128]{3,2,1,0:T(8,128)(2,1)} %bitcast.100, pred[4,28]{1,0:T(4,128)(4,1)S(1)} %get-tuple-element.227, f32[4,192,28,192]{1,3,2,0:T(8,128)} %copy-done, ...), kind=kOutput, calls=%fused_computation.20.clone.1 | convolution fusion | flops 1076428800 | bytes 22225924 | tf_op jit(solution)/shard_map/while/body/eval_jaxpr/while/body/eval_jaxpr/iqsk,iskd->iqd/dot_general | solution.py:42
  388.8 7.2 %fusion.56 = (f32[4,192]{1,0:T(4,128)S(1)}, f32[4,192,28,192]{1,3,2,0:T(8,128)S(1)}) fusion(pred[4,28]{1,0:T(4,128)(4,1)S(1)} %dynamic-slice_bitcast_fusion.2, bf16[4,28,192,128]{3,2,1,0:T(8,128)(2,1)} %bitcast.101, pred[4,28]{1,0:T(4,128)(4,1)S(1)} %get-tuple-element.227, bf16[2,4,192,128]{3,2,1,0:T(8,128)(2,1)S(1)} %get-tuple-element.249, ...), kind=kOutput, calls=%fused_computation.4.clone.1 | convolution fusion | flops 1072102656 | bytes 22220804 | tf_op jit(solution)/shard_map/while/body/eval_jaxpr/while/body/eval_jaxpr/iqd,iskd->iqsk/dot_general | solution.py:33
  396.0 5.7 %fusion.57 = f32[4,192]{1,0:T(4,128)S(1)} fusion(f32[4,192,28,192]{1,3,2,0:T(8,128)S(1)} %get-tuple-element.228, f32[4,192]{1,0:T(4,128)S(1)} %get-tuple-element.229, pred[4,28]{1,0:T(4,128)(4,1)S(1)} %dynamic-slice_bitcast_fusion.2), kind=kLoop, calls=%fused_computation.5.clone.1 | loop fusion | flops 16514304 | bytes 16521328 | tf_op jit(solution)/shard_map/while/body/eval_jaxpr/while/body/eval_jaxpr/reduce_sum | solution.py:39
  403.3 5.5 %gather_fusion = bf16[112,192,128]{2,1,0:T(8,128)(2,1)} fusion(bf16[48,192,128]{2,1,0:T(8,128)(2,1)} %get-tuple-element.252, s32[1024]{0:T(1024)S(1)} %pad_clamp_fusion.2), kind=kCustom, calls=%fused_computation.1.clone.clone.1 | custom fusion | bytes 11010496 | tf_op jit(solution)/shard_map/while/body/eval_jaxpr/while/body/eval_jaxpr/jit(_take)/gather | solution.py:31
  408.8 12.0 %fusion.58 = bf16[2,4,192,128]{3,2,1,0:T(8,128)(2,1)S(1)} fusion(bf16[2,4,192,128]{3,2,1,0:T(8,128)(2,1)S(1)} %copy-done.3, s32[]{:T(128)} %get-tuple-element.238, bf16[4,28,192,128]{3,2,1,0:T(8,128)(2,1)} %bitcast.100, pred[4,28]{1,0:T(4,128)(4,1)S(1)} %get-tuple-element.227, f32[4,192,28,192]{1,3,2,0:T(8,128)} %copy-done, ...), kind=kOutput, calls=%fused_computation.20.clone.1 | convolution fusion | flops 1076428800 | bytes 22225924 | tf_op jit(solution)/shard_map/while/body/eval_jaxpr/while/body/eval_jaxpr/iqsk,iskd->iqd/dot_general | solution.py:42
  423.4 6.7 %copy.48 = bf16[2,1536,128]{2,0,1:T(2,128)(2,1)S(1)} copy(bf16[2,1536,128]{2,1,0:T(8,128)(2,1)} %get-tuple-element.80) | data formatting | bytes 1572864 | tf_op jit(solution)/shard_map/while | solution.py:81
  430.1 28.7 %all_to_all.84 = bf16[1,1536,1,2,128]{4,3,2,0,1:T(2,128)(2,1)S(1)} all-to-all(bf16[1,1536,1,2,128]{4,3,2,0,1:T(2,128)(2,1)S(1)} %bitcast.108), channel_id=1, replica_groups=mesh['seq'=16,'cfg'=16] {'seq'}, dimensions={1} | all-to-all | bytes 1572864 | tf_op jit(solution)/shard_map/all_to_all | solution.py:102
  466.3 22.9 %all_to_all.85 = bf16[16,2,12288]{2,1,0:T(2,128)(2,1)S(1)} all-to-all(bf16[16,2,12288]{2,1,0:T(2,128)(2,1)S(1)} %reshape.91), channel_id=1, replica_groups=mesh['seq'=16,'cfg'=16] {'cfg'}, dimensions={0} | all-to-all | bytes 1572864 | tf_op jit(solution)/shard_map/all_to_all | solution.py:104
  497.1 20.4 %all_to_all.86 = bf16[16,6,4096]{2,1,0:T(8,128)(2,1)S(1)} all-to-all(bf16[16,6,4096]{2,1,0:T(8,128)(2,1)S(1)} %copy.38), channel_id=1, replica_groups=mesh['seq'=16,'cfg'=16] {'cfg'}, dimensions={0} | all-to-all | bytes 1572864 | tf_op jit(solution)/shard_map/all_to_all | solution.py:106
  (98 shorter events, 71.3 us)
Async XLA Ops:
  3.7 29.8 %all-to-all-start = ((bf16[1,96,16,2,128]{4,1,3,0,2:T(8,128)(2,1)}), bf16[1,96,16,2,128]{4,1,3,0,2:T(8,128)(2,1)S(1)}, u32[]{:S(2)}, u32[]{:S(2)}) async-start(bf16[1,96,16,2,128]{4,1,3,0,2:T(8,128)(2,1)} %copy.27), calls=%async_computation | async-start | bytes 1572864 | tf_op jit(solution)/shard_map/all_to_all | solution.py:85
  33.6 112.3 %all-to-all-start.1 = ((bf16[1,576,16,2,128]{4,1,3,0,2:T(8,128)(2,1)}), bf16[1,576,16,2,128]{4,1,3,0,2:T(8,128)(2,1)}, u32[]{:S(2)}, u32[]{:S(2)}) async-start(bf16[1,576,16,2,128]{4,1,3,0,2:T(8,128)(2,1)} %copy.29), calls=%async_computation.1 | async-start | bytes 9437184 | tf_op jit(solution)/shard_map/all_to_all | solution.py:90
  54.9 99.9 %copy-start.6 = (s32[8,28]{1,0:T(8,128)S(1)}, s32[8,28]{1,0:T(8,128)}, u32[]{:S(2)}) copy-start(s32[8,28]{1,0:T(8,128)} %param.15) | copy-start | bytes 2692
  145.9 114.9 %all-to-all-start.2 = ((bf16[1,576,16,2,128]{4,1,3,0,2:T(8,128)(2,1)}), bf16[1,576,16,2,128]{4,1,3,0,2:T(8,128)(2,1)}, u32[]{:S(2)}, u32[]{:S(2)}) async-start(bf16[1,576,16,2,128]{4,1,3,0,2:T(8,128)(2,1)} %copy.31), calls=%async_computation.2 | async-start | bytes 9437184 | tf_op jit(solution)/shard_map/all_to_all | solution.py:95
  265.6 3.6 copy-start.5
  269.3 3.9 copy-start.1
  280.4 7.3 %copy-start = (f32[4,192,28,192]{1,3,2,0:T(8,128)}, f32[4,192,28,192]{1,3,2,0:T(8,128)S(1)}, u32[]{:S(2)}) copy-start(f32[4,192,28,192]{1,3,2,0:T(8,128)S(1)} %get-tuple-element.228) | copy-start | bytes 49545220 | tf_op jit(solution)/shard_map/while/body/eval_jaxpr/while
  287.7 5.5 %copy-start.3 = (bf16[2,4,192,128]{3,2,1,0:T(8,128)(2,1)S(1)}, bf16[2,4,192,128]{3,2,1,0:T(8,128)(2,1)}, u32[]{:S(2)}) copy-start(bf16[2,4,192,128]{3,2,1,0:T(8,128)(2,1)} %get-tuple-element.239) | copy-start | bytes 1179652 | tf_op jit(solution)/shard_map/while/body/eval_jaxpr/while
  293.2 12.8 %copy-start.2 = (bf16[48,192,128]{2,1,0:T(8,128)(2,1)S(1)}, bf16[48,192,128]{2,1,0:T(8,128)(2,1)}, u32[]{:S(2)}) copy-start(bf16[48,192,128]{2,1,0:T(8,128)(2,1)} %copy-done.1) | copy-start | bytes 7077892 | tf_op jit(solution)/shard_map/while/body/eval_jaxpr/while
  305.2 0.8 copy-start.4
  306.0 3.9 copy-start.1
  317.1 7.3 %copy-start = (f32[4,192,28,192]{1,3,2,0:T(8,128)}, f32[4,192,28,192]{1,3,2,0:T(8,128)S(1)}, u32[]{:S(2)}) copy-start(f32[4,192,28,192]{1,3,2,0:T(8,128)S(1)} %get-tuple-element.228) | copy-start | bytes 49545220 | tf_op jit(solution)/shard_map/while/body/eval_jaxpr/while
  324.4 5.5 %copy-start.3 = (bf16[2,4,192,128]{3,2,1,0:T(8,128)(2,1)S(1)}, bf16[2,4,192,128]{3,2,1,0:T(8,128)(2,1)}, u32[]{:S(2)}) copy-start(bf16[2,4,192,128]{3,2,1,0:T(8,128)(2,1)} %get-tuple-element.239) | copy-start | bytes 1179652 | tf_op jit(solution)/shard_map/while/body/eval_jaxpr/while
  329.9 12.8 %copy-start.2 = (bf16[48,192,128]{2,1,0:T(8,128)(2,1)S(1)}, bf16[48,192,128]{2,1,0:T(8,128)(2,1)}, u32[]{:S(2)}) copy-start(bf16[48,192,128]{2,1,0:T(8,128)(2,1)} %copy-done.1) | copy-start | bytes 7077892 | tf_op jit(solution)/shard_map/while/body/eval_jaxpr/while
  342.0 0.8 copy-start.4
  344.5 3.6 copy-start.5
  348.1 3.9 copy-start.1
  359.3 7.3 %copy-start = (f32[4,192,28,192]{1,3,2,0:T(8,128)}, f32[4,192,28,192]{1,3,2,0:T(8,128)S(1)}, u32[]{:S(2)}) copy-start(f32[4,192,28,192]{1,3,2,0:T(8,128)S(1)} %get-tuple-element.228) | copy-start | bytes 49545220 | tf_op jit(solution)/shard_map/while/body/eval_jaxpr/while
  366.6 5.5 %copy-start.3 = (bf16[2,4,192,128]{3,2,1,0:T(8,128)(2,1)S(1)}, bf16[2,4,192,128]{3,2,1,0:T(8,128)(2,1)}, u32[]{:S(2)}) copy-start(bf16[2,4,192,128]{3,2,1,0:T(8,128)(2,1)} %get-tuple-element.239) | copy-start | bytes 1179652 | tf_op jit(solution)/shard_map/while/body/eval_jaxpr/while
  372.1 12.8 %copy-start.2 = (bf16[48,192,128]{2,1,0:T(8,128)(2,1)S(1)}, bf16[48,192,128]{2,1,0:T(8,128)(2,1)}, u32[]{:S(2)}) copy-start(bf16[48,192,128]{2,1,0:T(8,128)(2,1)} %copy-done.1) | copy-start | bytes 7077892 | tf_op jit(solution)/shard_map/while/body/eval_jaxpr/while
  384.1 0.8 copy-start.4
  384.9 3.9 copy-start.1
  396.0 7.3 %copy-start = (f32[4,192,28,192]{1,3,2,0:T(8,128)}, f32[4,192,28,192]{1,3,2,0:T(8,128)S(1)}, u32[]{:S(2)}) copy-start(f32[4,192,28,192]{1,3,2,0:T(8,128)S(1)} %get-tuple-element.228) | copy-start | bytes 49545220 | tf_op jit(solution)/shard_map/while/body/eval_jaxpr/while
  403.3 5.5 %copy-start.3 = (bf16[2,4,192,128]{3,2,1,0:T(8,128)(2,1)S(1)}, bf16[2,4,192,128]{3,2,1,0:T(8,128)(2,1)}, u32[]{:S(2)}) copy-start(bf16[2,4,192,128]{3,2,1,0:T(8,128)(2,1)} %get-tuple-element.239) | copy-start | bytes 1179652 | tf_op jit(solution)/shard_map/while/body/eval_jaxpr/while
  408.8 12.8 %copy-start.2 = (bf16[48,192,128]{2,1,0:T(8,128)(2,1)S(1)}, bf16[48,192,128]{2,1,0:T(8,128)(2,1)}, u32[]{:S(2)}) copy-start(bf16[48,192,128]{2,1,0:T(8,128)(2,1)} %copy-done.1) | copy-start | bytes 7077892 | tf_op jit(solution)/shard_map/while/body/eval_jaxpr/while
  420.9 0.8 copy-start.4
  460.2 34.7 %copy-start.7 = (f32[16]{0:T(128)S(1)}, f32[16]{0:T(128)}, u32[]{:S(2)}) copy-start(f32[16]{0:T(128)} %param.16) | copy-start | bytes 196
  460.2 34.7 %copy-start.8 = (s32[16]{0:T(128)S(1)}, s32[16]{0:T(128)}, u32[]{:S(2)}) copy-start(s32[16]{0:T(128)} %param.17) | copy-start | bytes 196
where the time goes:
time: 520 us; the launch traced here: 519 us
  waiting for transfers between devices  196 us (38%)
  local copies, waits for them, and re-layouts  118 us (23%)
  matrix products  78.8 us (15%)
  blocking collectives  72 us (14%)
  other arithmetic  28.3 us (5%)
  starting transfers between devices  25.3 us (5%)
    all_to_all x1, waiting for transfers between devices, body(): lax.all_to_all(split_heads(value_states), 'seq', split_axis=2, concat_axi...  100 us
    all_to_all x1, waiting for transfers between devices, body(): lax.all_to_all(split_heads(key_states), 'seq', split_axis=2, concat_axis=...  90.9 us
    dot_general x4, matrix products, tile_block(): jnp.einsum('iqsk,iskd->iqd', weights, value_block, preferred_element_type...  48.1 us
    reshape x6, local copies, waits for them, and re-layouts, split_heads(): return states.reshape(1, states.shape[1], seq_count, heads_here, head_size)  33.9 us
    dot_general x4, matrix products, tile_block(): jnp.einsum('iqd,iskd->iqsk', query_block, key_block, preferred_element_ty...  28.9 us
    all_to_all x1, blocking collectives, body(): lax.all_to_all(attended, 'seq', split_axis=1, concat_axis=2, tiled=True)  28.7 us
    all_to_all x1, blocking collectives, body(): lax.all_to_all(flattened, 'cfg', split_axis=1, concat_axis=0, tiled=True)  22.9 us
    reduce_sum x4, other arithmetic, tile_block(): totals = jnp.sum(exponent, axis=(2, 3))  22.8 us
  transfers between devices with their start and end apart: 3, of which 3 were waited for; matrix products, arithmetic and copies ran while one was open for 7% of the time, Pallas kernels for 0%

commit v1 on v0

v1 whole, which is shorter than its diff:
```python
import functools
import math

import jax
import jax.numpy as jnp
from jax import lax
from jax.experimental import pallas as pl
from jax.experimental.pallas import tpu as pltpu
from jax.sharding import PartitionSpec as P

MESH = pl.DeviceIdType.MESH
HEAD = 128
TILE = 192
RING = 8
NEG = -1e30
BIG = 1e30
NT = (((1,), (1,)), ((), ()))


def kernel(
    pattern, strength, partner, q_hbm, k_hbm, v_hbm, out,
    kb, vb, qb, qbd, vt, scores, probs, valid, own, own_lse,
    stage, stage_lse, got, got_lse, att, comb, sel, gst,
    k_sem, v_sem, q_sem, ag_sem, rs_sem, lse_sem, comb_sem, out_sem,
    ks_send, vs_send, qs_send, ag_send, rs_send, lse_send, att_send, gst_send,
):
    seq = lax.axis_index("seq")
    cfg = lax.axis_index("cfg")
    x = lax.div(seq, RING)
    z = lax.rem(seq, RING)
    ox = 1 - x
    pairs = kb.shape[0]
    rows = kb.shape[1] // 2
    qrows = q_hbm.shape[1]
    width = 2 * HEAD
    half = pairs * width
    lanes = 2 * TILE
    members = comb.shape[1]
    factor = math.log2(math.e) / math.sqrt(HEAD)

    def ring(a):
        return lax.rem(a + 2 * RING, RING)

    def remote(src, dst, send, recv, to_seq, to_cfg):
        return pltpu.make_async_remote_copy(
            src_ref=src, dst_ref=dst, send_sem=send, recv_sem=recv,
            device_id={"seq": to_seq, "cfg": to_cfg}, device_id_type=MESH,
        )

    def wait(ref, sem):
        pltpu.make_async_copy(ref, ref, sem).wait()

    barrier = pltpu.get_barrier_semaphore()

    def greet(to_seq, to_cfg):
        pl.semaphore_signal(
            barrier, inc=1, device_id={"seq": to_seq, "cfg": to_cfg}, device_id_type=MESH
        )

    greet(x * RING + ring(z + 1), cfg)
    greet(x * RING + ring(z - 1), cfg)
    for step in range(1, members):
        greet(seq, lax.rem(cfg + step, members))
    for step in range(members):
        greet(ox * RING + z, lax.rem(cfg + step, members))

    def local(p):
        cols = pl.ds(pl.multiple_of(x * half + p * width, width), width)
        mine = pl.ds(pl.multiple_of(x * rows, 64), rows)
        pltpu.make_async_copy(k_hbm.at[0, :, cols], kb.at[p, mine], k_sem.at[p]).start()
        pltpu.make_async_copy(v_hbm.at[0, :, cols], vb.at[p, mine], v_sem.at[p]).start()

    def local_q(p):
        cols = pl.ds(pl.multiple_of(x * half + p * width, width), width)
        mine = pl.ds(pl.multiple_of(x * qrows, 32), qrows)
        pltpu.make_async_copy(q_hbm.at[0, :, cols], qb.at[p, z, mine], q_sem.at[p]).start()

    def swap_kv(p):
        cols = pl.ds(pl.multiple_of(ox * half + p * width, width), width)
        mine = pl.ds(pl.multiple_of(x * rows, 64), rows)
        to = ox * RING + z
        remote(k_hbm.at[0, :, cols], kb.at[p, mine], ks_send, k_sem.at[p], to, cfg).start()
        remote(v_hbm.at[0, :, cols], vb.at[p, mine], vs_send, v_sem.at[p], to, cfg).start()

    def swap_q(p):
        cols = pl.ds(pl.multiple_of(ox * half + p * width, width), width)
        mine = pl.ds(pl.multiple_of(x * qrows, 32), qrows)
        to = ox * RING + z
        remote(q_hbm.at[0, :, cols], qb.at[p, z, mine], qs_send, q_sem.at[p], to, cfg).start()

    for p in range(pairs):
        local_q(p)
    for p in range(pairs):
        local(p)

    for s in range(6):
        tile = 3 * z + (s % 3) + (0 if s < 3 else 3 * RING)
        hit = jnp.max((pattern[...] == tile).astype(jnp.float32), axis=1, keepdims=True)
        lane = lax.broadcasted_iota(jnp.int32, (1, lanes), 1)
        first = lax.rem(lane, TILE) < qrows
        for b in range(RING):
            valid[b, s : s + 1, :] = jnp.where(
                first, hit[b // 2 : b // 2 + 1, :], hit[4 + b // 2 : 5 + b // 2, :]
            )

    qbd[...] = jnp.zeros_like(qbd)
    vt[width : width + 16, :] = jnp.ones((16, vt.shape[1]), vt.dtype)

    pl.semaphore_wait(barrier, 2 + (members - 1) + members)

    swap_q(0)
    swap_q(1)
    swap_kv(0)
    swap_q(2)
    swap_q(3)
    swap_kv(1)
    swap_q(4)
    swap_kv(2)

    def sign(p):
        return 1 - 2 * lax.rem(p, 2)

    def gather_send(p, step):
        sg = sign(p)
        block = qb.at[p, ring(z - sg * step)]
        remote(block, block, ag_send, ag_sem.at[p, step], x * RING + ring(z + sg), cfg).start()
        if step < 3:
            block = qb.at[p, ring(z + sg * step)]
            remote(
                block, block, ag_send, ag_sem.at[p, 4 + step], x * RING + ring(z - sg), cfg
            ).start()

    def gather_wait(p, step):
        sg = sign(p)
        wait(qb.at[p, ring(z - sg * (step + 1))], ag_sem.at[p, step])
        if step < 3:
            wait(qb.at[p, ring(z + sg * (step + 1))], ag_sem.at[p, 4 + step])

    def turn_values(p):
        vt[0:width, :] = vb[p].T

    def compute(p, j):
        sg = -sign(p)
        b0 = ring(z + sg * (4 - j))
        b1 = ring(z - sg * (3 - j))
        for n, b in enumerate((b0, b1)):
            qbd[n * lanes : n * lanes + TILE, 0:HEAD] = qb[p, b, :, 0:HEAD]
            qbd[n * lanes + TILE : (n + 1) * lanes, HEAD:width] = qb[p, b, :, HEAD:width]
        top = jnp.full((1, 2 * lanes), NEG, jnp.float32)
        for s in range(6):
            part = lax.dot_general(
                kb[p, s * TILE : (s + 1) * TILE, :], qbd[...], NT,
                preferred_element_type=jnp.float32,
            )
            scores[s * TILE : (s + 1) * TILE, :] = part
            here = jnp.max(part, axis=0, keepdims=True)
            ok = jnp.concatenate([valid[b0, s : s + 1, :], valid[b1, s : s + 1, :]], axis=1)
            top = jnp.maximum(top, jnp.where(ok > 0.0, here, NEG))
        for s in range(6):
            ok = jnp.concatenate([valid[b0, s : s + 1, :], valid[b1, s : s + 1, :]], axis=1)
            shift = jnp.where(ok > 0.0, top, BIG)
            probs[s * TILE : (s + 1) * TILE, :] = jnp.exp2(
                (scores[s * TILE : (s + 1) * TILE, :] - shift) * factor
            ).astype(jnp.bfloat16)
        both = jnp.dot(vt[...], probs[...], preferred_element_type=jnp.float32)
        total = both[width : width + 1, :]
        some = total > 0.0
        safe = jnp.where(some, total, 1.0)
        lse = jnp.where(some, top * factor + jnp.log2(safe), NEG)
        scale = jnp.where(some, 1.0 / safe, 0.0)
        lane = lax.broadcasted_iota(jnp.int32, (1, 2 * lanes), 1)
        first = lax.rem(lane, lanes) < TILE
        o = jnp.where(first, both[0:HEAD, :], both[HEAD:width, :]) * scale
        slot = lax.rem(p, 3)
        for n in range(2):
            own[slot, 2 * j + n] = o[:, n * lanes : (n + 1) * lanes]
            own_lse[slot, 2 * j + n] = lse[:, n * lanes : (n + 1) * lanes]

    def merge(oa, la, ob, lb):
        m = jnp.maximum(la, lb)
        wa = jnp.exp2(la - m)
        wb = jnp.exp2(lb - m)
        t = wa + wb
        r = 1.0 / t
        return oa * (wa * r) + ob * (wb * r), m + jnp.log2(t)

    def reduce_send(p, step):
        sg = -sign(p)
        slot = lax.rem(p, 3)
        chains = ((0, step, 2 * step, z + sg),)
        if step < 3:
            chains += ((1, 4 + step, 2 * step + 1, z - sg),)
        for _, at, mine, to in chains:
            o = own[slot, mine]
            lse = own_lse[slot, mine]
            if step > 0:
                wait(got.at[p, at - 1], rs_sem.at[p, at - 1])
                wait(got_lse.at[p, at - 1], lse_sem.at[p, at - 1])
                o, lse = merge(
                    o, lse, got[p, at - 1].astype(jnp.float32), got_lse[p, at - 1]
                )
            stage[p, at] = o.astype(jnp.bfloat16)
            stage_lse[p, at] = lse
            there = x * RING + ring(to)
            remote(stage.at[p, at], got.at[p, at], rs_send, rs_sem.at[p, at], there, cfg).start()
            remote(
                stage_lse.at[p, at], got_lse.at[p, at], lse_send, lse_sem.at[p, at], there, cfg
            ).start()

    def finish(p):
        slot = lax.rem(p, 3)
        o = own[slot, 7]
        lse = own_lse[slot, 7]
        for at in (6, 3):
            wait(got.at[p, at], rs_sem.at[p, at])
            wait(got_lse.at[p, at], lse_sem.at[p, at])
            o, lse = merge(o, lse, got[p, at].astype(jnp.float32), got_lse[p, at])
        turned = o.T.astype(jnp.bfloat16)
        g = lax.div(p, 2)
        e = lax.rem(p, 2)
        for c in range(8):
            att[g, e * 8 + c] = turned[c * 48 : (c + 1) * 48, :]

    def spread(g):
        pltpu.make_async_copy(att.at[g, cfg], comb.at[g, cfg], comb_sem.at[g]).start()
        for step in range(1, members):
            c = lax.rem(cfg + step, members)
            remote(att.at[g, c], comb.at[g, cfg], att_send, comb_sem.at[g], seq, c).start()

    def combine(g):
        wait(comb.at[g], comb_sem.at[g])
        sel[...] = comb[g]
        hh = lax.div(cfg, 4)
        tx = lax.rem(lax.div(cfg, 2), 2)
        start = pl.multiple_of(lax.rem(cfg, 2) * 48, 16)
        cols = pl.ds(pl.multiple_of(x * half + g * 2 * width + hh * HEAD, HEAD), HEAD)
        for m in range(members):
            a = sel[m].astype(jnp.float32)
            other = sel[partner[m]].astype(jnp.float32)
            gst[g, m] = (other + strength[m] * (a - other)).astype(jnp.bfloat16)
        for step in range(members):
            m = lax.rem(cfg + step, members)
            there = remote(
                gst.at[g, m], out.at[0, pl.ds(start, 48), cols], gst_send, out_sem,
                tx * RING + z, m,
            )
            if step == 0:
                here = pltpu.make_async_copy(
                    gst.at[g, m], out.at[0, pl.ds(start, 48), cols], out_sem
                )

                @pl.when(tx == x)
                def _():
                    here.start()

                @pl.when(tx != x)
                def _():
                    there.start()

            else:
                there.start()

    def body(t, carry):
        i = t - 2
        ahead2 = (i + 2 < pairs)
        ahead1 = (i + 1 >= 0) & (i + 1 < pairs)
        now = (i >= 0) & (i < pairs)
        behind1 = (i >= 1) & (i < pairs + 1)
        behind2 = (i >= 2) & (i < pairs + 2)

        @pl.when(ahead2)
        def _():
            wait(qb.at[i + 2, z], q_sem.at[i + 2])
            gather_send(i + 2, 0)

        @pl.when(ahead1)
        def _():
            gather_wait(i + 1, 1)
            gather_send(i + 1, 2)

        @pl.when(now)
        def _():
            gather_wait(i, 3)
            wait(kb.at[i], k_sem.at[i])
            wait(vb.at[i], v_sem.at[i])

            @pl.when(i + 3 < pairs)
            def _():
                swap_kv(i + 3)

            @pl.when(i + 5 < pairs)
            def _():
                swap_q(i + 5)

            turn_values(i)
            lax.fori_loop(0, 2, lambda j, c: (compute(i, j), c)[1], 0)
            reduce_send(i, 0)

        @pl.when(behind1)
        def _():
            reduce_send(i - 1, 2)

        @pl.when(behind2)
        def _():
            finish(i - 2)

            @pl.when(lax.rem(i, 2) == 1)
            def _():
                spread(lax.div(i - 3, 2))

        @pl.when(ahead2)
        def _():
            gather_wait(i + 2, 0)
            gather_send(i + 2, 1)

        @pl.when(ahead1)
        def _():
            gather_wait(i + 1, 2)
            gather_send(i + 1, 3)

        @pl.when(now)
        def _():
            lax.fori_loop(2, 4, lambda j, c: (compute(i, j), c)[1], 0)
            reduce_send(i, 1)

        @pl.when(behind1)
        def _():
            reduce_send(i - 1, 3)

        @pl.when((i >= 4) & (lax.rem(i + 2, 2) == 0))
        def _():
            combine(lax.div(i - 4, 2))

        return carry

    lax.fori_loop(0, pairs + 5, body, 0)

    wait(out.at[0], out_sem)
    wait(kb.at[:, 0:rows], ks_send)
    wait(vb.at[:, 0:rows], vs_send)
    wait(qb.at[:, 0, 0:qrows], qs_send)
    wait(qb.at[:, 0:7], ag_send)
    wait(stage, rs_send)
    wait(stage_lse, lse_send)
    wait(att.at[:, 0 : members - 1], att_send)
    tx = lax.rem(lax.div(cfg, 2), 2)

    @pl.when(tx == x)
    def _():
        wait(gst.at[:, 0 : members - 1], gst_send)

    @pl.when(tx != x)
    def _():
        wait(gst, gst_send)


def body(query_states, key_states, value_states, tile_pattern, strength, partner):
    rows = key_states.shape[1]
    qrows = query_states.shape[1]
    pairs = query_states.shape[2] // (4 * HEAD)
    members = lax.axis_size("cfg")
    width, lanes = 2 * HEAD, 2 * TILE
    bf, f32 = jnp.bfloat16, jnp.float32
    vm = pltpu.VMEM
    dma = pltpu.SemaphoreType.DMA
    return pl.pallas_call(
        kernel,
        out_shape=jax.ShapeDtypeStruct(query_states.shape, bf),
        in_specs=[
            pl.BlockSpec(memory_space=pltpu.VMEM),
            pl.BlockSpec(memory_space=pltpu.SMEM),
            pl.BlockSpec(memory_space=pltpu.SMEM),
            pl.BlockSpec(memory_space=pl.ANY),
            pl.BlockSpec(memory_space=pl.ANY),
            pl.BlockSpec(memory_space=pl.ANY),
        ],
        out_specs=pl.BlockSpec(memory_space=pl.ANY),
        scratch_shapes=[
            vm((pairs, 2 * rows, width), bf),
            vm((pairs, 2 * rows, width), bf),
            vm((pairs, RING, 2 * qrows, width), bf),
            vm((2 * lanes, width), bf),
            vm((width + 16, 2 * rows), bf),
            vm((2 * rows, 2 * lanes), f32),
            vm((2 * rows, 2 * lanes), bf),
            vm((RING, 8, lanes), f32),
            vm((3, 8, HEAD, lanes), f32),
            vm((3, 8, 1, lanes), f32),
            vm((pairs, 7, HEAD, lanes), bf),
            vm((pairs, 7, 1, lanes), f32),
            vm((pairs, 7, HEAD, lanes), bf),
            vm((pairs, 7, 1, lanes), f32),
            vm((pairs // 2, members, 48, HEAD), bf),
            vm((pairs // 2, members, 48, HEAD), bf),
            vm((members, 48, HEAD), bf),
            vm((pairs // 2, members, 48, HEAD), bf),
            dma((pairs,)),
            dma((pairs,)),
            dma((pairs,)),
            dma((pairs, 7)),
            dma((pairs, 7)),
            dma((pairs, 7)),
            dma((pairs // 2,)),
            dma,
            dma,
            dma,
            dma,
            dma,
            dma,
            dma,
            dma,
            dma,
        ],
        compiler_params=pltpu.CompilerParams(
            collective_id=0, has_side_effects=True, vmem_limit_bytes=60 * 1024 * 1024
        ),
        cost_estimate=pl.CostEstimate(
            flops=30_000_000_000, bytes_accessed=24_000_000, transcendentals=28_000_000
        ),
    )(tile_pattern, strength, partner, query_states, key_states, value_states)


def solution(mesh):
    return jax.shard_map(
        body,
        mesh=mesh,
        in_specs=(
            P("cfg", "seq", None),
            P("cfg", "seq", None),
            P("cfg", "seq", None),
            P(),
            P(),
            P(),
        ),
        out_specs=P("cfg", "seq", None),
        check_vma=False,
    )
```

time: 520 us -> 177 us (0.34)
  waiting for transfers between devices: 196 us -> 0 us
  Pallas kernels: 0 us -> 175 us
  local copies, waits for them, and re-layouts: 118 us -> 2.06 us
  matrix products: 78.8 us -> 0 us
  blocking collectives: 72 us -> 0 us
  other arithmetic: 28.3 us -> 0 us
  starting transfers between devices: 25.3 us -> 0 us
    all_to_all x3 -> x0, waiting for transfers between devices: 196 us -> none  [the longest x1 100 us: body(): lax.all_to_all(split_heads(value_states), 'seq', split_axis=2, concat_axi...]
    pallas_call x0 -> x1, Pallas kernels: none -> 175 us  [body(): pl.pallas_call(kernel, out_shape=jax.ShapeDtypeStruct(query_states.shape,...]
    dot_general x9 -> x0, matrix products: 78.8 us -> none  [the longest x4 48.1 us: tile_block(): jnp.einsum('iqsk,iskd->iqd', weights, value_block, preferred_element_type...]
    all_to_all x3 -> x0, blocking collectives: 72 us -> none  [the longest x1 28.7 us: body(): lax.all_to_all(attended, 'seq', split_axis=1, concat_axis=2, tiled=True)]
    gather x8 -> x0, local copies, waits for them, and re-layouts: 37 us -> none  [the longest x4 22 us: tile_block(): value_block = jnp.take(value_tiles, index_block, axis=0)]
    reshape x7 -> x0, local copies, waits for them, and re-layouts: 34.3 us -> none  [the longest x6 33.9 us: split_heads(): return states.reshape(1, states.shape[1], seq_count, heads_here, head_size)]
    all_to_all x3 -> x0, starting transfers between devices: 25.3 us -> none  [the longest x1 10 us: body(): lax.all_to_all(split_heads(query_states), 'seq', split_axis=2, concat_axi...]
    reduce_sum x4 -> x0, other arithmetic: 22.8 us -> none  [tile_block(): totals = jnp.sum(exponent, axis=(2, 3))]
  transfers between devices with their start and end apart: 3 -> 0, of which waited for: 3 -> 0; matrix products, arithmetic and copies ran while one was open for 7% -> 0% of each run, Pallas kernels for 0% -> 0%
where the time goes in v1:
time: 177 us
  Pallas kernels  175 us (99%)
  local copies, waits for them, and re-layouts  2.06 us (1%)
    pallas_call x1, Pallas kernels, body(): pl.pallas_call(kernel, out_shape=jax.ShapeDtypeStruct(query_states.shape,...  175 us

profile of v1, /device:TPU:1, one launch (start us, length us, event | category | flops | bytes accessed | tf_op | source)
XLA Modules:
  0.0 177.3 jit_solution(3279182194115441435)
XLA Ops:
  0.0 175.2 %shard_map.64 = bf16[1,96,4096]{2,1,0:T(8,128)(2,1)} custom-call(s32[8,28]{1,0:T(8,128)} %pattern.1, f32[16]{0:T(128)} %strength.1, s32[16]{0:T(128)} %partner.1, bf16[1,96,4096]{2,1,0:T(8,128)(2,1)} %q_hbm.1, bf16[1,576,4096]{2,1,0:T(8,128)(2,1)} %k_hbm.1, bf16[1,576,4096]{2,1,0:T(8,128)(2,1)} %v_hbm.1), custom_call_target="tpu_custom_call" | custom-call | flops 30000001024 | bytes 24000000 | tf_op jit(solution)/shard_map/pallas_call | solution.py:366
  175.2 2.1 %copy.8 = bf16[1,96,4096]{2,1,0:T(8,128)(2,1)} copy(bf16[1,96,4096]{2,1,0:T(8,128)(2,1)} %shard_map.64) | data formatting | bytes 1572864

commit v2 on v1

--- a/solution.py
+++ b/solution.py
@@ -14,6 +14,8 @@
 RING = 8
 NEG = -1e30
 BIG = 1e30
+DEPTH = 2
+LEAD = 12
 NT = (((1,), (1,)), ((), ()))
 
 
@@ -29,6 +31,8 @@
     x = lax.div(seq, RING)
     z = lax.rem(seq, RING)
     ox = 1 - x
+    hi = lax.rem(lax.div(cfg, 2), 2)
+    hx = lax.rem(x + hi, 2)
     pairs = kb.shape[0]
     rows = kb.shape[1] // 2
     qrows = q_hbm.shape[1]
@@ -60,30 +64,35 @@
     greet(x * RING + ring(z + 1), cfg)
     greet(x * RING + ring(z - 1), cfg)
     for step in range(1, members):
-        greet(seq, lax.rem(cfg + step, members))
+        c = lax.rem(cfg + step, members)
+
+        @pl.when(lax.rem(lax.div(c, 2), 2) == hi)
+        def _():
+            greet(seq, c)
+
     for step in range(members):
         greet(ox * RING + z, lax.rem(cfg + step, members))
 
     def local(p):
-        cols = pl.ds(pl.multiple_of(x * half + p * width, width), width)
+        cols = pl.ds(pl.multiple_of(hx * half + p * width, width), width)
         mine = pl.ds(pl.multiple_of(x * rows, 64), rows)
         pltpu.make_async_copy(k_hbm.at[0, :, cols], kb.at[p, mine], k_sem.at[p]).start()
         pltpu.make_async_copy(v_hbm.at[0, :, cols], vb.at[p, mine], v_sem.at[p]).start()
 
     def local_q(p):
-        cols = pl.ds(pl.multiple_of(x * half + p * width, width), width)
+        cols = pl.ds(pl.multiple_of(hx * half + p * width, width), width)
         mine = pl.ds(pl.multiple_of(x * qrows, 32), qrows)
         pltpu.make_async_copy(q_hbm.at[0, :, cols], qb.at[p, z, mine], q_sem.at[p]).start()
 
     def swap_kv(p):
-        cols = pl.ds(pl.multiple_of(ox * half + p * width, width), width)
+        cols = pl.ds(pl.multiple_of((1 - hx) * half + p * width, width), width)
         mine = pl.ds(pl.multiple_of(x * rows, 64), rows)
         to = ox * RING + z
         remote(k_hbm.at[0, :, cols], kb.at[p, mine], ks_send, k_sem.at[p], to, cfg).start()
         remote(v_hbm.at[0, :, cols], vb.at[p, mine], vs_send, v_sem.at[p], to, cfg).start()
 
     def swap_q(p):
-        cols = pl.ds(pl.multiple_of(ox * half + p * width, width), width)
+        cols = pl.ds(pl.multiple_of((1 - hx) * half + p * width, width), width)
         mine = pl.ds(pl.multiple_of(x * qrows, 32), qrows)
         to = ox * RING + z
         remote(q_hbm.at[0, :, cols], qb.at[p, z, mine], qs_send, q_sem.at[p], to, cfg).start()
@@ -106,16 +115,12 @@
     qbd[...] = jnp.zeros_like(qbd)
     vt[width : width + 16, :] = jnp.ones((16, vt.shape[1]), vt.dtype)
 
-    pl.semaphore_wait(barrier, 2 + (members - 1) + members)
+    pl.semaphore_wait(barrier, 2 + (members // 2 - 1) + members)
 
     swap_q(0)
     swap_q(1)
+    swap_q(2)
     swap_kv(0)
-    swap_q(2)
-    swap_q(3)
-    swap_kv(1)
-    swap_q(4)
-    swap_kv(2)
 
     def sign(p):
         return 1 - 2 * lax.rem(p, 2)
@@ -124,7 +129,9 @@
         sg = sign(p)
         block = qb.at[p, ring(z - sg * step)]
         remote(block, block, ag_send, ag_sem.at[p, step], x * RING + ring(z + sg), cfg).start()
-        if step < 3:
+
+        @pl.when(step < 3)
+        def _():
             block = qb.at[p, ring(z + sg * step)]
             remote(
                 block, block, ag_send, ag_sem.at[p, 4 + step], x * RING + ring(z - sg), cfg
@@ -133,7 +140,9 @@
     def gather_wait(p, step):
         sg = sign(p)
         wait(qb.at[p, ring(z - sg * (step + 1))], ag_sem.at[p, step])
-        if step < 3:
+
+        @pl.when(step < 3)
+        def _():
             wait(qb.at[p, ring(z + sg * (step + 1))], ag_sem.at[p, 4 + step])
 
     def turn_values(p):
@@ -184,28 +193,41 @@
         r = 1.0 / t
         return oa * (wa * r) + ob * (wb * r), m + jnp.log2(t)
 
+    def chain_send(p, at, o, lse, to):
+        stage[p, at] = o.astype(jnp.bfloat16)
+        stage_lse[p, at] = lse
+        there = x * RING + ring(to)
+        remote(stage.at[p, at], got.at[p, at], rs_send, rs_sem.at[p, at], there, cfg).start()
+        remote(
+            stage_lse.at[p, at], got_lse.at[p, at], lse_send, lse_sem.at[p, at], there, cfg
+        ).start()
+
+    def chain_merge(p, at, mine):
+        slot = lax.rem(p, 3)
+        wait(got.at[p, at], rs_sem.at[p, at])
+        wait(got_lse.at[p, at], lse_sem.at[p, at])
+        return merge(
+            own[slot, mine], own_lse[slot, mine], got[p, at].astype(jnp.float32), got_lse[p, at]
+        )
+
     def reduce_send(p, step):
         sg = -sign(p)
         slot = lax.rem(p, 3)
-        chains = ((0, step, 2 * step, z + sg),)
-        if step < 3:
-            chains += ((1, 4 + step, 2 * step + 1, z - sg),)
-        for _, at, mine, to in chains:
-            o = own[slot, mine]
-            lse = own_lse[slot, mine]
-            if step > 0:
-                wait(got.at[p, at - 1], rs_sem.at[p, at - 1])
-                wait(got_lse.at[p, at - 1], lse_sem.at[p, at - 1])
-                o, lse = merge(
-                    o, lse, got[p, at - 1].astype(jnp.float32), got_lse[p, at - 1]
-                )
-            stage[p, at] = o.astype(jnp.bfloat16)
-            stage_lse[p, at] = lse
-            there = x * RING + ring(to)
-            remote(stage.at[p, at], got.at[p, at], rs_send, rs_sem.at[p, at], there, cfg).start()
-            remote(
-                stage_lse.at[p, at], got_lse.at[p, at], lse_send, lse_sem.at[p, at], there, cfg
-            ).start()
+
+        @pl.when(step == 0)
+        def _():
+            chain_send(p, 0, own[slot, 0], own_lse[slot, 0], z + sg)
+            chain_send(p, 4, own[slot, 1], own_lse[slot, 1], z - sg)
+
+        @pl.when(step > 0)
+        def _():
+            o, lse = chain_merge(p, step - 1, 2 * step)
+            chain_send(p, step, o, lse, z + sg)
+
+        @pl.when((step > 0) & (step < 3))
+        def _():
+            o, lse = chain_merge(p, 3 + step, 2 * step + 1)
+            chain_send(p, 4 + step, o, lse, z - sg)
 
     def finish(p):
         slot = lax.rem(p, 3)
@@ -221,119 +243,101 @@
         for c in range(8):
             att[g, e * 8 + c] = turned[c * 48 : (c + 1) * 48, :]
 
+    def share(c):
+        lo = lax.rem(hx + lax.rem(lax.div(c, 2), 2), 2)
+        return lo, lax.div(c, 4) * 4 + (1 - lo) * 2 + lax.rem(c, 2)
+
     def spread(g):
-        pltpu.make_async_copy(att.at[g, cfg], comb.at[g, cfg], comb_sem.at[g]).start()
+        _, mine = share(cfg)
+        pltpu.make_async_copy(att.at[g, mine], comb.at[g, cfg], comb_sem.at[g]).start()
         for step in range(1, members):
             c = lax.rem(cfg + step, members)
-            remote(att.at[g, c], comb.at[g, cfg], att_send, comb_sem.at[g], seq, c).start()
+            lo, which = share(c)
+            remote(
+                att.at[g, which], comb.at[g, cfg], att_send, comb_sem.at[g], lo * RING + z, c
+            ).start()
 
     def combine(g):
         wait(comb.at[g], comb_sem.at[g])
         sel[...] = comb[g]
         hh = lax.div(cfg, 4)
-        tx = lax.rem(lax.div(cfg, 2), 2)
         start = pl.multiple_of(lax.rem(cfg, 2) * 48, 16)
-        cols = pl.ds(pl.multiple_of(x * half + g * 2 * width + hh * HEAD, HEAD), HEAD)
+        cols = pl.ds(pl.multiple_of(hx * half + g * 2 * width + hh * HEAD, HEAD), HEAD)
         for m in range(members):
             a = sel[m].astype(jnp.float32)
             other = sel[partner[m]].astype(jnp.float32)
             gst[g, m] = (other + strength[m] * (a - other)).astype(jnp.bfloat16)
         for step in range(members):
             m = lax.rem(cfg + step, members)
-            there = remote(
+            remote(
                 gst.at[g, m], out.at[0, pl.ds(start, 48), cols], gst_send, out_sem,
-                tx * RING + z, m,
-            )
-            if step == 0:
-                here = pltpu.make_async_copy(
-                    gst.at[g, m], out.at[0, pl.ds(start, 48), cols], out_sem
-                )
-
-                @pl.when(tx == x)
-                def _():
-                    here.start()
-
-                @pl.when(tx != x)
-                def _():
-                    there.start()
-
-            else:
-                there.start()
-
-    def body(t, carry):
-        i = t - 2
-        ahead2 = (i + 2 < pairs)
-        ahead1 = (i + 1 >= 0) & (i + 1 < pairs)
+                ox * RING + z, m,
+            ).start()
+
+    def body(u, carry):
+        t = u - LEAD
+        i = lax.div(t + 16, 4) - 4
+        j = lax.rem(t + 16, 4)
+        hop = lax.rem(4 - j, 4)
+        back = lax.div(t - 3 * hop + 32, 4) - 8
+        ahead = back + 3
         now = (i >= 0) & (i < pairs)
-        behind1 = (i >= 1) & (i < pairs + 1)
-        behind2 = (i >= 2) & (i < pairs + 2)
-
-        @pl.when(ahead2)
-        def _():
-            wait(qb.at[i + 2, z], q_sem.at[i + 2])
-            gather_send(i + 2, 0)
-
-        @pl.when(ahead1)
-        def _():
-            gather_wait(i + 1, 1)
-            gather_send(i + 1, 2)
+
+        @pl.when((ahead >= 0) & (ahead < pairs))
+        def _():
+            @pl.when(hop == 0)
+            def _():
+                wait(qb.at[ahead, z], q_sem.at[ahead])
+
+            @pl.when(hop > 0)
+            def _():
+                gather_wait(ahead, hop - 1)
+
+            gather_send(ahead, hop)
+
+        @pl.when(j == 0)
+        def _():
+            @pl.when((i >= -2) & (i + 5 < pairs))
+            def _():
+                swap_q(i + 5)
+
+            @pl.when(now)
+            def _():
+                wait(kb.at[i], k_sem.at[i])
+                wait(vb.at[i], v_sem.at[i])
+
+            @pl.when((i >= 1 - DEPTH) & (i + DEPTH < pairs))
+            def _():
+                swap_kv(i + DEPTH)
+
+            @pl.when(now)
+            def _():
+                gather_wait(i, 3)
+                turn_values(i)
 
         @pl.when(now)
         def _():
-            gather_wait(i, 3)
-            wait(kb.at[i], k_sem.at[i])
-            wait(vb.at[i], v_sem.at[i])
-
-            @pl.when(i + 3 < pairs)
-            def _():
-                swap_kv(i + 3)
-
-            @pl.when(i + 5 < pairs)
-            def _():
-                swap_q(i + 5)
-
-            turn_values(i)
-            lax.fori_loop(0, 2, lambda j, c: (compute(i, j), c)[1], 0)
-            reduce_send(i, 0)
-
-        @pl.when(behind1)
-        def _():
-            reduce_send(i - 1, 2)
-
-        @pl.when(behind2)
-        def _():
-            finish(i - 2)
-
-            @pl.when(lax.rem(i, 2) == 1)
-            def _():
-                spread(lax.div(i - 3, 2))
-
-        @pl.when(ahead2)
-        def _():
-            gather_wait(i + 2, 0)
-            gather_send(i + 2, 1)
-
-        @pl.when(ahead1)
-        def _():
-            gather_wait(i + 1, 2)
-            gather_send(i + 1, 3)
-
-        @pl.when(now)
-        def _():
-            lax.fori_loop(2, 4, lambda j, c: (compute(i, j), c)[1], 0)
-            reduce_send(i, 1)
-
-        @pl.when(behind1)
-        def _():
-            reduce_send(i - 1, 3)
-
-        @pl.when((i >= 4) & (lax.rem(i + 2, 2) == 0))
-        def _():
-            combine(lax.div(i - 4, 2))
+            compute(i, j)
+
+        @pl.when((back >= 0) & (back < pairs))
+        def _():
+            reduce_send(back, hop)
+
+        @pl.when((j == 0) & (i >= 3) & (i - 3 < pairs))
+        def _():
+            finish(i - 3)
+
+            @pl.when(lax.rem(i, 2) == 0)
+            def _():
+                spread(lax.div(i - 4, 2))
+
+        @pl.when((t >= 19) & (lax.rem(t + 32 - 19, 8) == 0))
+        def _():
+            combine(lax.div(t - 19, 8))
 
         return carry
 
-    lax.fori_loop(0, pairs + 5, body, 0)
+    lax.fori_loop(0, LEAD + 4 * (pairs - 1) + 16, body, 0)
 
     wait(out.at[0], out_sem)
     wait(kb.at[:, 0:rows], ks_send)
@@ -343,15 +347,7 @@
     wait(stage, rs_send)
     wait(stage_lse, lse_send)
     wait(att.at[:, 0 : members - 1], att_send)
-    tx = lax.rem(lax.div(cfg, 2), 2)
-
-    @pl.when(tx == x)
-    def _():
-        wait(gst.at[:, 0 : members - 1], gst_send)
-
-    @pl.when(tx != x)
-    def _():
-        wait(gst, gst_send)
+    wait(gst, gst_send)
 
 
 def body(query_states, key_states, value_states, tile_pattern, strength, partner):

time: 177 us -> 160 us (0.904)
  Pallas kernels: 175 us -> 158 us
    pallas_call x1, Pallas kernels: 175 us -> 158 us  [body(): pl.pallas_call(kernel, out_shape=jax.ShapeDtypeStruct(query_states.shape,...]
where the time goes in v2:
time: 160 us
  Pallas kernels  158 us (99%)
  local copies, waits for them, and re-layouts  2.06 us (1%)
    pallas_call x1, Pallas kernels, body(): pl.pallas_call(kernel, out_shape=jax.ShapeDtypeStruct(query_states.shape,...  158 us

profile of v2, /device:TPU:1, one launch (start us, length us, event | category | flops | bytes accessed | tf_op | source)
XLA Modules:
  0.0 159.9 jit_solution(808955495997318721)
XLA Ops:
  0.0 157.8 %shard_map.64 = bf16[1,96,4096]{2,1,0:T(8,128)(2,1)} custom-call(s32[8,28]{1,0:T(8,128)} %pattern.1, f32[16]{0:T(128)} %strength.1, s32[16]{0:T(128)} %partner.1, bf16[1,96,4096]{2,1,0:T(8,128)(2,1)} %q_hbm.1, bf16[1,576,4096]{2,1,0:T(8,128)(2,1)} %k_hbm.1, bf16[1,576,4096]{2,1,0:T(8,128)(2,1)} %v_hbm.1), custom_call_target="tpu_custom_call" | custom-call | flops 30000001024 | bytes 24000000 | tf_op jit(solution)/shard_map/pallas_call | solution.py:362
  157.8 2.1 %copy.8 = bf16[1,96,4096]{2,1,0:T(8,128)(2,1)} copy(bf16[1,96,4096]{2,1,0:T(8,128)(2,1)} %shard_map.64) | data formatting | bytes 1572864

commit v3 on v2

--- a/solution.py
+++ b/solution.py
@@ -117,9 +117,8 @@
 
     pl.semaphore_wait(barrier, 2 + (members // 2 - 1) + members)
 
-    swap_q(0)
-    swap_q(1)
-    swap_q(2)
+    for p in range(pairs):
+        swap_q(p)
     swap_kv(0)
 
     def sign(p):
@@ -137,6 +136,10 @@
                 block, block, ag_send, ag_sem.at[p, 4 + step], x * RING + ring(z - sg), cfg
             ).start()
 
+    def gather_start(p):
+        wait(qb.at[p, z], q_sem.at[p])
+        gather_send(p, 0)
+
     def gather_wait(p, step):
         sg = sign(p)
         wait(qb.at[p, ring(z - sg * (step + 1))], ag_sem.at[p, step])
@@ -149,7 +152,7 @@
         vt[0:width, :] = vb[p].T
 
     def compute(p, j):
-        sg = -sign(p)
+        sg = sign(p)
         b0 = ring(z + sg * (4 - j))
         b1 = ring(z - sg * (3 - j))
         for n, b in enumerate((b0, b1)):
@@ -211,7 +214,7 @@
         )
 
     def reduce_send(p, step):
-        sg = -sign(p)
+        sg = sign(p)
         slot = lax.rem(p, 3)
 
         @pl.when(step == 0)
@@ -247,26 +250,35 @@
         lo = lax.rem(hx + lax.rem(lax.div(c, 2), 2), 2)
         return lo, lax.div(c, 4) * 4 + (1 - lo) * 2 + lax.rem(c, 2)
 
-    def spread(g):
-        _, mine = share(cfg)
-        pltpu.make_async_copy(att.at[g, mine], comb.at[g, cfg], comb_sem.at[g]).start()
-        for step in range(1, members):
-            c = lax.rem(cfg + step, members)
+    def spread(p):
+        g = lax.div(p, 2)
+        e = lax.rem(p, 2)
+        for step in range(members // 2):
+            c = e * (members // 2) + lax.rem(cfg + step, members // 2)
             lo, which = share(c)
-            remote(
-                att.at[g, which], comb.at[g, cfg], att_send, comb_sem.at[g], lo * RING + z, c
-            ).start()
+
+            @pl.when(c == cfg)
+            def _():
+                pltpu.make_async_copy(att.at[g, which], comb.at[g, cfg], comb_sem.at[g]).start()
+
+            @pl.when(c != cfg)
+            def _():
+                remote(
+                    att.at[g, which], comb.at[g, cfg], att_send, comb_sem.at[g], lo * RING + z, c
+                ).start()
 
     def combine(g):
         wait(comb.at[g], comb_sem.at[g])
         sel[...] = comb[g]
-        hh = lax.div(cfg, 4)
-        start = pl.multiple_of(lax.rem(cfg, 2) * 48, 16)
-        cols = pl.ds(pl.multiple_of(hx * half + g * 2 * width + hh * HEAD, HEAD), HEAD)
         for m in range(members):
             a = sel[m].astype(jnp.float32)
             other = sel[partner[m]].astype(jnp.float32)
             gst[g, m] = (other + strength[m] * (a - other)).astype(jnp.bfloat16)
+
+    def give(g):
+        hh = lax.div(cfg, 4)
+        start = pl.multiple_of(lax.rem(cfg, 2) * 48, 16)
+        cols = pl.ds(pl.multiple_of(hx * half + g * 2 * width + hh * HEAD, HEAD), HEAD)
         for step in range(members):
             m = lax.rem(cfg + step, members)
             remote(
@@ -283,24 +295,17 @@
         ahead = back + 3
         now = (i >= 0) & (i < pairs)
 
-        @pl.when((ahead >= 0) & (ahead < pairs))
-        def _():
-            @pl.when(hop == 0)
-            def _():
-                wait(qb.at[ahead, z], q_sem.at[ahead])
-
-            @pl.when(hop > 0)
-            def _():
-                gather_wait(ahead, hop - 1)
-
+        @pl.when((hop > 0) & (ahead >= 0) & (ahead < pairs))
+        def _():
+            gather_wait(ahead, hop - 1)
             gather_send(ahead, hop)
 
+        @pl.when((hop == 0) & (ahead + 1 < pairs))
+        def _():
+            gather_start(ahead + 1)
+
         @pl.when(j == 0)
         def _():
-            @pl.when((i >= -2) & (i + 5 < pairs))
-            def _():
-                swap_q(i + 5)
-
             @pl.when(now)
             def _():
                 wait(kb.at[i], k_sem.at[i])
@@ -315,28 +320,35 @@
                 gather_wait(i, 3)
                 turn_values(i)
 
+        active = (back >= 0) & (back < pairs)
+
         @pl.when(now)
         def _():
             compute(i, j)
 
-        @pl.when((back >= 0) & (back < pairs))
+        @pl.when(active)
         def _():
             reduce_send(back, hop)
 
         @pl.when((j == 0) & (i >= 3) & (i - 3 < pairs))
         def _():
             finish(i - 3)
-
-            @pl.when(lax.rem(i, 2) == 0)
-            def _():
-                spread(lax.div(i - 4, 2))
+            spread(i - 3)
 
         @pl.when((t >= 19) & (lax.rem(t + 32 - 19, 8) == 0))
         def _():
             combine(lax.div(t - 19, 8))
 
+        last = 4 * pairs
+        for g, slot in enumerate((last, last + 1, last + 3, last + 11)):
+
+            @pl.when(t == slot)
+            def _():
+                give(g)
+
         return carry
 
+    gather_start(0)
     lax.fori_loop(0, LEAD + 4 * (pairs - 1) + 16, body, 0)
 
     wait(out.at[0], out_sem)

time: 160 us -> 158 us (0.988); the launches traced: 160 us -> 156 us
  Pallas kernels: 158 us -> 154 us
    pallas_call x1, Pallas kernels: 158 us -> 154 us  [body(): pl.pallas_call(kernel, out_shape=jax.ShapeDtypeStruct(query_states.shape,...]
where the time goes in v3:
time: 158 us; the launch traced here: 156 us
  Pallas kernels  154 us (97%)
  local copies, waits for them, and re-layouts  2.06 us (1%)
    pallas_call x1, Pallas kernels, body(): pl.pallas_call(kernel, out_shape=jax.ShapeDtypeStruct(query_states.shape,...  154 us

profile of v3, /device:TPU:1, one launch (start us, length us, event | category | flops | bytes accessed | tf_op | source)
XLA Modules:
  0.0 156.0 jit_solution(11880885422787901016)
XLA Ops:
  0.0 153.9 %shard_map.64 = bf16[1,96,4096]{2,1,0:T(8,128)(2,1)} custom-call(s32[8,28]{1,0:T(8,128)} %pattern.1, f32[16]{0:T(128)} %strength.1, s32[16]{0:T(128)} %partner.1, bf16[1,96,4096]{2,1,0:T(8,128)(2,1)} %q_hbm.1, bf16[1,576,4096]{2,1,0:T(8,128)(2,1)} %k_hbm.1, bf16[1,576,4096]{2,1,0:T(8,128)(2,1)} %v_hbm.1), custom_call_target="tpu_custom_call" | custom-call | flops 30000001024 | bytes 24000000 | tf_op jit(solution)/shard_map/pallas_call | solution.py:374
  153.9 2.1 %copy.8 = bf16[1,96,4096]{2,1,0:T(8,128)(2,1)} copy(bf16[1,96,4096]{2,1,0:T(8,128)(2,1)} %shard_map.64) | data formatting | bytes 1572864
